TPU v7x, 32 devices: a whole 2x2x4 slice. The times are simulated.
32 devices in a mesh: pole: 2 (over y), prow: 1, pcol: 16 (over z, x, core).
Axes of the slice: x: 2, y: 2, z: 4, core: 2. Of those that a mesh axis runs over, the one named last changes fastest.
Arguments:
- anc_inverse: float32 [12288, 6144], P(('pole', 'prow'), 'pcol'), parts along dimension 0, may hold values from -8 to 8
- anc_factor: float32 [12288, 768], P(('pole', 'pcol')), parts along dimension 0, may hold values from -0.078125 to 0.078125
- win_factor: float32 [1536, 768], P('pole'), parts along dimension 0, may hold values from -0.375 to 0.375
- pivot_inverse: float32 [6, 256, 256], P('pole'), parts along dimension 0, may hold values from -6 to 6
- structure: int32 [3, 24], replicated, may hold values 0 or 1
Outputs:
- anc_columns: float32 [12288, 768], P(('pole', 'prow', 'pcol')), parts along dimension 0
- win_inverse: float32 [1536, 768], P('pole'), parts along dimension 0
There are 2 independent parts, one for each index of `pole`. A program takes and returns all parts, laid end to end along the dimension named above; an argument that names none is the same for every part. Nothing has to cross between parts.
All inputs are finite; a program needn't handle non-finite values.
Results may differ from a plain program's by a relative error of at most 0.0001.
Values sent between devices are 32-bit elements; how exact they have to be, the bound alone decides.
A program may use at most 128 MiB of HBM per device.

v0:
```python
import functools

import jax
import jax.numpy as jnp
from jax import lax
from jax.experimental import pallas as pl
from jax.experimental.pallas import tpu as pltpu
from jax.sharding import PartitionSpec as P

MESH = pl.DeviceIdType.MESH
UP, DOWN, ACROSS, MATE = range(4)
Z = 4
LANES = 8


def split(value):
    high = value.astype(jnp.bfloat16)
    low = (value - high.astype(jnp.float32)).astype(jnp.bfloat16)
    return high, low


def dot3(left, right):
    (lh, ll), (rh, rl) = left, right
    dot = functools.partial(jnp.dot, preferred_element_type=jnp.float32)
    return dot(lh, rh) + (dot(lh, rl) + dot(ll, rh))


def mul(left, right):
    return dot3(split(left), split(right))


def fused_kernel(steps, width, anc_ref, fac_ref, win_ref, piv_ref, str_ref, cols_ref, out_ref, *scratch):
    (gath, fac_st, anc_st, win_st, piv_st, tr_hi, tr_lo, acc, pivot_rest) = scratch[:9]
    parts = scratch[9 : 9 + steps]
    mates = scratch[9 + steps : 9 + 2 * steps]
    halves = scratch[9 + 2 * steps : 9 + 3 * steps]
    slots = scratch[9 + 3 * steps : 9 + 4 * steps]
    sums = scratch[9 + 4 * steps : 9 + 5 * steps]
    (load_sem, send_sem, recv_sem, s1, r1, s2, r2, s3, r3, s4, r4) = scratch[9 + 5 * steps :]

    me = lax.axis_index("pcol")
    core = lax.rem(me, 2)
    x = lax.rem(me // 2, 2)
    z = me // 4
    lane = me // 2
    rows = fac_st.shape[0]
    half = width // 2
    piece = half // LANES
    mate = me + 1 - 2 * core

    def index(zz, xx, cc):
        return (zz * 2 + xx) * 2 + cc

    across = index(z, 1 - x, core)

    load_fac = pltpu.make_async_copy(fac_ref, fac_st, load_sem.at[0])
    load_anc = pltpu.make_async_copy(anc_ref, anc_st, load_sem.at[1])
    load_win = pltpu.make_async_copy(win_ref, win_st, load_sem.at[2])
    load_piv = pltpu.make_async_copy(piv_ref, piv_st, load_sem.at[3])
    load_fac.start()

    barrier = pltpu.get_barrier_semaphore()
    for d in range(1, LANES):
        peer = lax.rem(lane + d, LANES) * 2 + core
        pl.semaphore_signal(barrier, inc=1, device_id={"pcol": peer}, device_id_type=MESH)
    pl.semaphore_signal(barrier, inc=1, device_id={"pcol": mate}, device_id_type=MESH)

    load_fac.wait()
    load_anc.start()
    load_win.start()
    load_piv.start()
    sub = width // 2

    def mask_own(k):
        for piece_at in range(rows // sub):
            block = (me * (rows // sub) + piece_at) // 2
            kept = str_ref[k, block].astype(jnp.float32)
            gath[k, me, piece_at * sub : (piece_at + 1) * sub, :] = (
                fac_st[piece_at * sub : (piece_at + 1) * sub, k * width : (k + 1) * width] * kept
            )

    mask_own(steps - 1)
    pl.semaphore_wait(barrier, LANES)

    def remote(kind, k, block, dest):
        return pltpu.make_async_remote_copy(
            src_ref=gath.at[k, block],
            dst_ref=gath.at[k, block],
            send_sem=send_sem.at[kind, k, block],
            recv_sem=recv_sem.at[k, block],
            device_id={"pcol": dest},
            device_id_type=MESH,
        )

    def order(t):
        inner = (0, 0, 2, 3) if t else (1, 1, 1, 1)
        lowmid = inner[t] if t else 1
        highmid = 3 - lowmid
        return jnp.where(z == 0, t, jnp.where(z == 1, lowmid, jnp.where(z == 2, highmid, 3 - t)))

    def column_sends(k, t, act):
        zz = order(t)
        block = index(zz, x, core)

        def vertical(kind, dest, cond):
            @pl.when(cond)
            def _():
                act(remote(kind, k, block, dest))

        if t == 0:
            vertical(UP, jnp.minimum(me + 4, 4 * Z - 1), z < Z - 1)
            vertical(DOWN, jnp.maximum(me - 4, 0), z > 0)
        else:
            vertical(UP, jnp.minimum(me + 4, 4 * Z - 1), (zz < z) & (z < Z - 1))
            vertical(DOWN, jnp.maximum(me - 4, 0), (zz > z) & (z > 0))
        act(remote(ACROSS, k, block, across))
        act(remote(MATE, k, block, mate))

    def arrived(k, block):
        remote(MATE, k, block, mate).wait_recv()

    def column_event(k, t):
        if t > 0:
            arrived(k, index(order(t), x, core))
        column_sends(k, t, lambda copy: copy.start())

    def across_event(k, t):
        block = index(order(t), 1 - x, core)
        arrived(k, block)
        remote(MATE, k, block, mate).start()

    def compute_event(k, t):
        zz = order(t)
        arrived(k, index(zz, x, 1 - core))
        arrived(k, index(zz, 1 - x, 1 - core))

        def body(i, carry):
            block = zz * 4 + i
            if k == steps - 1:
                tile = anc_st[pl.ds(pl.multiple_of(block * rows, rows), rows), :].T
                high, low = split(tile)
                tr_hi[block] = high
                tr_lo[block] = low
            else:
                high, low = tr_hi[block], tr_lo[block]
            term = dot3((high, low), split(gath[k, block]))
            acc[...] += term
            return carry

        if t == 0:
            start = jnp.zeros(acc.shape, jnp.float32)
            for j in range(k + 1, steps):
                start = start + mul(cols_ref[:, j * width : (j + 1) * width], fac_block(j, k))
            acc[...] = start
        lax.fori_loop(0, 4, body, 0)

    def fac_block(j, k):
        return win_st[j * width : (j + 1) * width, k * width : (k + 1) * width]

    def finish(k):
        column = -acc[...]
        cols_ref[:, k * width : (k + 1) * width] = column
        flipped = split(column.T)
        for i in range(k + 1):
            parts[k][:, i * width : (i + 1) * width] = dot3(flipped, split(gath[i, me]))

    def mate_copy(k):
        return pltpu.make_async_remote_copy(
            src_ref=parts[k].at[pl.ds(pl.multiple_of((1 - core) * half, half), half), :],
            dst_ref=mates[k],
            send_sem=s1.at[k],
            recv_sem=r1.at[k],
            device_id={"pcol": mate},
            device_id_type=MESH,
        )

    def scatter_copy(k, d):
        peer = lax.rem(lane + d, LANES)
        return pltpu.make_async_remote_copy(
            src_ref=halves[k].at[pl.ds(pl.multiple_of(peer * piece, piece), piece), :],
            dst_ref=slots[k].at[lane],
            send_sem=s2.at[k, peer],
            recv_sem=r2.at[k, lane],
            device_id={"pcol": peer * 2 + core},
            device_id_type=MESH,
        )

    def scatter_wait(k, d):
        peer = lax.rem(lane + d, LANES)
        pltpu.make_async_remote_copy(
            src_ref=slots[k].at[peer],
            dst_ref=slots[k].at[peer],
            send_sem=s2.at[k, peer],
            recv_sem=r2.at[k, peer],
            device_id={"pcol": peer * 2 + core},
            device_id_type=MESH,
        ).wait_recv()

    def spread_copy(k, d, owner):
        peer = lax.rem(lane + d, LANES)
        at = pl.ds(pl.multiple_of(core * half + owner * piece, piece), piece)
        return pltpu.make_async_remote_copy(
            src_ref=sums[k].at[at, :],
            dst_ref=sums[k].at[at, :],
            send_sem=s3.at[k, peer],
            recv_sem=r3.at[k, owner],
            device_id={"pcol": peer * 2 + core},
            device_id_type=MESH,
        )

    def join_copy(k, which):
        at = pl.ds(pl.multiple_of(which * half, half), half)
        return pltpu.make_async_remote_copy(
            src_ref=sums[k].at[at, :],
            dst_ref=sums[k].at[at, :],
            send_sem=s4.at[k],
            recv_sem=r4.at[k],
            device_id={"pcol": mate},
            device_id_type=MESH,
        )

    def phase(k, number):
        if number == 1:
            mate_copy(k).start()
        elif number == 2:
            mate_copy(k).wait_recv()
            own = pl.ds(pl.multiple_of(core * half, half), half)
            halves[k][...] = parts[k][own, :] + mates[k][...]
            for d in range(1, LANES):
                scatter_copy(k, d).start()
        elif number == 3:
            total = halves[k][pl.ds(pl.multiple_of(lane * piece, piece), piece), :]
            for d in range(1, LANES):
                scatter_wait(k, d)
                total = total + slots[k][lax.rem(lane + d, LANES)]
            sums[k][pl.ds(pl.multiple_of(core * half + lane * piece, piece), piece), :] = total
            for d in range(1, LANES):
                spread_copy(k, d, lane).start()
        elif number == 4:
            for d in range(1, LANES):
                spread_copy(k, d, lax.rem(lane + d, LANES)).wait_recv()
            join_copy(k, core).start()
        else:
            join_copy(k, 1 - core).wait_recv()
            window(k)

    def put(j, k, value):
        out_ref[j * width : (j + 1) * width, k * width : (k + 1) * width] = value

    def got(j, k):
        return out_ref[j * width : (j + 1) * width, k * width : (k + 1) * width]

    def summed(j, k):
        return sums[j][:, k * width : (k + 1) * width]

    def window(k):
        if k == 0:
            put(0, 0, pivot_rest[...] - summed(0, 0).T)
            return
        diag = piv_st[k] - summed(k, k).T
        for j in range(k + 1, steps):
            diag = diag - mul(fac_block(j, k).T, got(j, k))
        put(k, k, diag)
        low = k - 1
        for j in range(k, steps):
            running = summed(j, low)
            for i in range(k, steps):
                running = running + mul(got(j, i), fac_block(i, low))
            put(j, low, -running)
            put(low, j, -running.T)
        if low == 0:
            rest = piv_st[0]
            for j in range(1, steps):
                rest = rest - mul(fac_block(j, 0).T, got(j, 0))
            pivot_rest[...] = rest

    events = [(k, t) for k in range(steps - 1, -1, -1) for t in range(Z)]
    lag_across, lag_compute = 1, 2
    pending = []
    for g in range(len(events) + lag_compute):
        if g < len(events):
            column_event(*events[g])
        if g == 0:
            for k in range(steps - 1):
                mask_own(k)
            load_anc.wait()
            load_win.wait()
            load_piv.wait()
        if 0 <= g - lag_across < len(events):
            across_event(*events[g - lag_across])
        for k, first in pending:
            number = g - first + 1
            if 2 <= number <= (5 if k > 1 else 4):
                phase(k, number)
        if g >= lag_compute:
            k, t = events[g - lag_compute]
            compute_event(k, t)
            if t == Z - 1:
                finish(k)
                phase(k, 1)
                pending.append((k, g))
    phase(0, 2)
    phase(1, 5)
    for number in range(3, 6):
        phase(0, number)

    for k, t in events:
        column_sends(k, t, lambda copy: copy.wait_send())
        remote(MATE, k, index(order(t), 1 - x, core), mate).wait_send()
    for k in range(steps):
        mate_copy(k).wait_send()
        for d in range(1, LANES):
            scatter_copy(k, d).wait_send()
            spread_copy(k, d, lane).wait_send()
        join_copy(k, core).wait_send()


def fused(anc_inverse, anc_factor, win_factor, pivot_inverse, structure):
    steps, width = pivot_inverse.shape[:2]
    rows, all_cols = anc_factor.shape
    devices = lax.axis_size("pcol")
    half = width // 2
    piece = half // LANES
    f32, b16 = jnp.float32, jnp.bfloat16
    wide = [(k + 1) * width for k in range(steps)]
    dma = pltpu.SemaphoreType.DMA
    scratch = [
        pltpu.VMEM((steps, devices, rows, width), f32),
        pltpu.VMEM((rows, all_cols), f32),
        pltpu.VMEM(anc_inverse.shape, f32),
        pltpu.VMEM(win_factor.shape, f32),
        pltpu.VMEM(pivot_inverse.shape, f32),
        pltpu.VMEM((devices, rows, rows), b16),
        pltpu.VMEM((devices, rows, rows), b16),
        pltpu.VMEM((rows, width), f32),
        pltpu.VMEM((width, width), f32),
        *[pltpu.VMEM((width, w), f32) for w in wide],
        *[pltpu.VMEM((half, w), f32) for w in wide],
        *[pltpu.VMEM((half, w), f32) for w in wide],
        *[pltpu.VMEM((LANES, piece, w), f32) for w in wide],
        *[pltpu.VMEM((width, w), f32) for w in wide],
        dma((4,)),
        dma((4, steps, devices)),
        dma((steps, devices)),
        dma((steps,)),
        dma((steps,)),
        dma((steps, LANES)),
        dma((steps, LANES)),
        dma((steps, LANES)),
        dma((steps, LANES)),
        dma((steps,)),
        dma((steps,)),
    ]
    whole = pl.BlockSpec(memory_space=pl.ANY)
    vmem = pl.BlockSpec(memory_space=pltpu.VMEM)
    return pl.pallas_call(
        functools.partial(fused_kernel, steps, width),
        out_shape=(
            jax.ShapeDtypeStruct((rows, all_cols), f32),
            jax.ShapeDtypeStruct((all_cols, all_cols), f32),
        ),
        in_specs=[whole, whole, whole, whole, pl.BlockSpec(memory_space=pltpu.SMEM)],
        out_specs=(vmem, vmem),
        scratch_shapes=scratch,
        compiler_params=pltpu.CompilerParams(
            collective_id=0, has_side_effects=True, vmem_limit_bytes=62 * 2**20
        ),
    )(anc_inverse, anc_factor, win_factor, pivot_inverse, structure)


precise = lax.Precision.HIGHEST


def product(left, right):
    return jnp.dot(left, right, precision=precise, preferred_element_type=jnp.float32)


def on_device(anc_inverse, anc_factor, win_factor, pivot_inverse, structure):
    row_count = lax.axis_size("prow")
    col_count = lax.axis_size("pcol")
    if row_count == 1 and col_count == 4 * Z and 2 * anc_factor.shape[0] == 3 * pivot_inverse.shape[1]:
        return fused(anc_inverse, anc_factor, win_factor, pivot_inverse, structure)
    row_index = lax.axis_index("prow")
    col_index = lax.axis_index("pcol")
    block_rows = anc_inverse.shape[0]
    block_cols = anc_inverse.shape[1]
    steps_total = pivot_inverse.shape[0]
    width = pivot_inverse.shape[1]
    all_cols = anc_factor.shape[1]
    block_count = structure.shape[1]
    ratio_cols = col_count // row_count
    share_rows = block_rows // col_count
    structure_cols = structure.T.astype(jnp.float32)
    global_rows = col_index * block_cols + lax.iota(jnp.int32, block_cols)
    onehot_rows = (
        (global_rows // width)[:, None] == lax.iota(jnp.int32, block_count)[None, :]
    ).astype(jnp.float32)
    kept_rows = product(onehot_rows, structure_cols)
    share_offset = col_index * share_rows
    share_global = (row_index * col_count + col_index) * share_rows + lax.iota(
        jnp.int32, share_rows
    )
    onehot_share = (
        (share_global // width)[:, None] == lax.iota(jnp.int32, block_count)[None, :]
    ).astype(jnp.float32)
    kept_share = product(onehot_share, structure_cols)
    slot_ids = lax.iota(jnp.int32, col_count)
    source_flag = (slot_ids // row_count == col_index - row_index * ratio_cols).astype(jnp.float32)
    pieces = jnp.tile(anc_factor.reshape(row_count, share_rows, all_cols), (ratio_cols, 1, 1))
    outgoing = pieces * source_flag[:, None, None]
    incoming = lax.all_to_all(outgoing, "pcol", split_axis=0, concat_axis=0, tiled=True)
    factor_share = jnp.sum(incoming, axis=0)
    column_store = {}
    share_store = {}
    window_blocks = {}
    for k in range(steps_total - 1, -1, -1):
        first_col = k * width
        factor_now = anc_factor[:, first_col : first_col + width] * kept_rows[:, k : k + 1]
        share_factor = factor_share[:, first_col : first_col + width] * kept_share[:, k : k + 1]
        finished = list(range(k + 1, steps_total))
        if finished:
            stacked = jnp.concatenate([column_store[j] for j in finished], axis=1)
            factor_win = win_factor[first_col + width :, first_col : first_col + width]

        def term_rows(start, count, factor_now=factor_now):
            return product(anc_inverse, factor_now)

        share_image = lax.psum_scatter(
            term_rows(jnp.int32(0), share_rows * lax.axis_size("pcol")),
            "pcol",
            scatter_dimension=0,
            tiled=True,
        )
        if finished:
            share_image = share_image + product(
                lax.dynamic_slice_in_dim(stacked, share_offset, share_rows, 0), factor_win
            )
        share_column = -share_image
        column_now = lax.all_gather(share_column, "pcol", axis=0, tiled=True)
        crossings = [product(share_store[j].T, share_factor) for j in finished]
        pivot_part = product(share_factor.T, share_column)
        cross_sums = []
        if finished:
            cross_total = lax.psum(jnp.stack(crossings), ("prow", "pcol"))
            cross_sums = [cross_total[position] for position in range(len(finished))]
        pivot_sum = lax.psum(pivot_part, ("prow", "pcol"))
        for position, j in enumerate(finished):
            running = cross_sums[position]
            for i in finished:
                running = running + product(
                    window_blocks[j, i],
                    win_factor[i * width : (i + 1) * width, first_col : first_col + width],
                )
            window_blocks[j, k] = -running
            window_blocks[k, j] = -running.T
        pivot_block = pivot_inverse[k] - pivot_sum
        for j in finished:
            pivot_block = pivot_block - product(
                win_factor[j * width : (j + 1) * width, first_col : first_col + width].T,
                window_blocks[j, k],
            )
        window_blocks[k, k] = pivot_block
        column_store[k] = column_now
        share_store[k] = share_column
    anc_columns = jnp.concatenate([share_store[k] for k in range(steps_total)], axis=1)
    win_inverse = jnp.concatenate(
        [
            jnp.concatenate([window_blocks[i, k] for k in range(steps_total)], axis=1)
            for i in range(steps_total)
        ],
        axis=0,
    )
    return (anc_columns, win_inverse)


def solution(mesh):
    in_specs = (
        P(("pole", "prow"), "pcol"),
        P(("pole", "pcol"), None),
        P("pole", None),
        P("pole", None, None),
        P(),
    )
    out_specs = (P(("pole", "prow", "pcol"), None), P("pole", None))
    return jax.shard_map(
        on_device, mesh=mesh, in_specs=in_specs, out_specs=out_specs, check_vma=False
    )
```

profile of v0, /device:TPU:1, one launch (start us, length us, event | category | flops | bytes accessed | tf_op | source)
XLA Modules:
  0.0 154.5 jit_solution(2086743151327012805)
XLA Ops:
  0.6 149.9 %shard_map.68 = (f32[384,768]{1,0:T(8,128)}, f32[768,768]{1,0:T(8,128)}) custom-call(f32[6144,384]{1,0:T(8,128)} %anc_ref.1, f32[384,768]{1,0:T(8,128)} %fac_ref.1, f32[768,768]{1,0:T(8,128)} %win_ref.1, f32[3,256,256]{2,1,0:T(8,128)} %piv_ref.1, s32[3,24]{1,0:T(4,128)} %str_ref.1), custom_call_target="tpu_custom_call" | custom-call | tf_op jit(solution)/shard_map/pallas_call | solution.py:356
  150.6 0.0 copy-start
  150.6 2.5 %copy.9 = f32[384,768]{1,0:T(8,128)} copy(f32[384,768]{1,0:T(8,128)} %get-tuple-element.4) | data formatting | bytes 2359296
  153.1 0.0 copy-done
  153.1 1.4 copy.10
Async XLA Ops:
  150.6 2.5 %copy-start = (f32[768,768]{1,0:T(8,128)S(1)}, f32[768,768]{1,0:T(8,128)}, u32[]{:S(2)}) copy-start(f32[768,768]{1,0:T(8,128)} %get-tuple-element.5) | copy-start | bytes 7077892
where the time goes:
time: 155 us
  Pallas kernels  150 us (97%)
  local copies, waits for them, and re-layouts  3.92 us (3%)
    pallas_call x1, Pallas kernels, fused(): pl.pallas_call(functools.partial(fused_kernel, steps, width), out_shape=(...  150 us
    unnamed x4, local copies, waits for them, and re-layouts  3.92 us

commit v1 on v0

v1 whole, which is shorter than its diff:
```python
import functools

import jax
import jax.numpy as jnp
from jax import lax
from jax.experimental import pallas as pl
from jax.experimental.pallas import tpu as pltpu
from jax.sharding import PartitionSpec as P

MESH = pl.DeviceIdType.MESH
UP, DOWN, ACROSS, MATE = range(4)
Z = 4
LANES = 8


def split(value):
    high = value.astype(jnp.bfloat16)
    low = (value - high.astype(jnp.float32)).astype(jnp.bfloat16)
    return high, low


def dot3(left, right):
    (lh, ll), (rh, rl) = left, right
    dot = functools.partial(jnp.dot, preferred_element_type=jnp.float32)
    return dot(lh, rh) + (dot(lh, rl) + dot(ll, rh))


def mul(left, right):
    return dot3(split(left), split(right))


STAGES = 2
SLOTS = 8


def item_list(u):
    if u == 0:
        rest = [("R1", 3), ("R0", 3), ("R1", 2), ("R0", 2), ("R1", 1), ("R0", 1)]
        return [("G", 0), ("H", 0)] + rest
    if u == 1:
        rest = [("R1", 3), ("R0", 3), ("R1", 2), ("R0", 2)]
        return [("G", 1), ("H", 1), ("G", 0), ("H", 0)] + rest
    rest = [("G", 1), ("H", 1), ("G", 0), ("H", 0), ("R1", 3), ("R0", 3)]
    return [("G", 2), ("H", 2)] + rest


def order_static(z):
    return ([0, 1, 2, 3], [1, 0, 2, 3], [2, 3, 1, 0], [3, 2, 1, 0])[z]


def fused_kernel(names, width, anc_ref, fac_ref, win_ref, piv_ref, str_ref, cols_ref, out_ref, *scratch):
    m = dict(zip(names, scratch, strict=True))
    fac, a_buf, win_st, piv_st = m["fac"], m["a_buf"], m["win"], m["piv"]
    lr_hi, lr_lo, lt_hi, lt_lo = m["lr_hi"], m["lr_lo"], m["lt_hi"], m["lt_lo"]
    tr_hi, tr_lo = m["tr_hi"], m["tr_lo"]
    own, near, y_own, y_near = m["own"], m["near"], m["y_own"], m["y_near"]
    p0, m0i, x0i, z0i = m["p0"], m["m0i"], m["x0i"], m["z0i"]
    p1, m1i, x1i, z1i = m["p1"], m["m1i"], m["x1i"], m["z1i"]

    me = lax.axis_index("pcol")
    core = lax.rem(me, 2)
    x = lax.rem(me // 2, 2)
    z = me // 4
    lane = me // 2
    rows = fac.shape[0]
    tile = width // 2
    mate = me + 1 - 2 * core

    def index(zz, xx, cc):
        return (zz * 2 + xx) * 2 + cc

    x_other = 1 - x
    across = index(z, x_other, core)

    def order(t):
        inner = (0, 0, 2, 3) if t else (1, 1, 1, 1)
        lowmid = inner[t] if t else 1
        highmid = 3 - lowmid
        return jnp.where(z == 0, t, jnp.where(z == 1, lowmid, jnp.where(z == 2, highmid, 3 - t)))

    def job_chip(q):
        return order(3 - q // 2) * 2 + (1 - x if q % 2 == 0 else x)

    def load_anc(q):
        at = pl.ds(pl.multiple_of(job_chip(q) * 2 * rows, 2 * rows), 2 * rows)
        return pltpu.make_async_copy(anc_ref.at[at, :], a_buf.at[q % 4], m["load_sem"].at[q])

    load_fac = pltpu.make_async_copy(fac_ref, fac, m["load_sem"].at[8])
    load_piv = pltpu.make_async_copy(piv_ref, piv_st, m["load_sem"].at[9])
    win_pairs = [(2, 1), (1, 0), (2, 0)]

    def load_win(n):
        j, k = win_pairs[n]
        block = win_ref.at[pl.ds(j * width, width), pl.ds(k * width, width)]
        return pltpu.make_async_copy(block, win_st.at[n], m["load_sem"].at[10 + n])

    load_fac.start()
    for q in range(4):
        load_anc(q).start()

    barrier = pltpu.get_barrier_semaphore()
    for d in range(1, LANES):
        peer = lax.rem(lane + d, LANES) * 2 + core
        pl.semaphore_signal(barrier, inc=1, device_id={"pcol": peer}, device_id_type=MESH)
    pl.semaphore_signal(barrier, inc=1, device_id={"pcol": mate}, device_id_type=MESH)

    common = []
    by_z = [[] for _ in range(Z)]
    log = [common]

    def go(make):
        make().start()
        log[0].append(make)

    def remote(src, dst, ssem, rsem, dest):
        return pltpu.make_async_remote_copy(
            src_ref=src, dst_ref=dst, send_sem=ssem, recv_sem=rsem, device_id={"pcol": dest}, device_id_type=MESH
        )

    def arrive(dst, rsem):
        remote(dst, dst, rsem, rsem, mate).wait_recv()

    def core_rows(c):
        return pl.ds(pl.multiple_of(c * rows, rows), rows)

    def own_at(s, zz, xx, c):
        return own.at[s, zz * 2 + xx, core_rows(c), :]

    def near_at(s, zz, c):
        return near.at[s, zz, core_rows(c), :]

    def own_send(s, zz, xx, kind, dest):
        def make():
            ref = own_at(s, zz, xx, core)
            return remote(ref, ref, m["own_s"].at[s, kind, zz * 2 + xx], m["own_r"].at[s, zz * 2 + xx, core], dest)
        go(make)

    def near_send(s, zz, kind, dest):
        def make():
            ref = near_at(s, zz, core)
            return remote(ref, ref, m["near_s"].at[s, kind, zz], m["near_r"].at[s, zz, core], dest)
        go(make)

    def own_wait(s, zz, xx, c):
        arrive(own_at(s, zz, xx, c), m["own_r"].at[s, zz * 2 + xx, c])

    def near_wait(s, zz, c):
        arrive(near_at(s, zz, c), m["near_r"].at[s, zz, c])

    def columns(t):
        return slice(t * tile, (t + 1) * tile)

    def mask(t):
        for piece in range(rows // tile):
            block = (me * (rows // tile) + piece) // 2
            kept = str_ref[t // 2, block].astype(jnp.float32)
            at = slice(piece * tile, (piece + 1) * tile)
            fac[at, columns(t)] = fac[at, columns(t)] * kept

    own_tiles, near_tiles, sum_tiles = (5, 2), (4, 1), (3, 0)

    load_fac.wait()
    mask(own_tiles[0])
    own[0, lane, core_rows(core), :] = fac[:, columns(own_tiles[0])]
    pl.semaphore_wait(barrier, LANES)

    def in_direction(direction, zz):
        return zz if direction == UP else Z - 1 - zz

    z_dests = (me + 4, me - 4)

    def z_dest(direction):
        return z_dests[direction]

    def landing(direction, zz, dest_z):
        return Z if direction == DOWN and dest_z == zz else dest_z

    def z_send(direction, zz, n):
        s, (kind, v) = n // SLOTS, item_list(in_direction(direction, zz))[n % SLOTS]
        vz = in_direction(direction, v)
        first = in_direction(direction, zz) == 0
        dest = z_dest(direction)
        there = zz + 1 if direction == UP else zz - 1
        if kind == "G":
            own_send(s, vz, x, direction, dest)
        elif kind == "H":
            near_send(s, vz, direction, dest)
        elif kind == "R1":
            arrive(m1i.at[s, vz], m["m1_r"].at[s, vz])
            value = p1[s, 0, vz] + m1i[s, vz]
            if not first:
                value = value + z1i[s, vz]
            p1[s, 0, vz] = value
            at = landing(direction, there, vz)
            go(lambda: remote(p1.at[s, 0, vz], z1i.at[s, at], m["z1_s"].at[s, vz], m["z1_r"].at[s, at], z_dest(direction)))
        else:
            arrive(m0i.at[s, 0, vz], m["m0_r"].at[s, 0, vz])
            arrive(x0i.at[s, vz], m["x0_r"].at[s, vz])
            value = p0[s, 0, 0, vz] + m0i[s, 0, vz] + x0i[s, vz]
            if not first:
                value = value + z0i[s, vz]
            p0[s, 0, 0, vz] = value
            at = landing(direction, there, vz)
            go(lambda: remote(p0.at[s, 0, 0, vz], z0i.at[s, at], m["z0_s"].at[s, vz], m["z0_r"].at[s, at], z_dest(direction)))

    def z_arrival(direction, zz, n):
        u = in_direction(direction, zz)
        s, (kind, v) = n // SLOTS, item_list(u - 1)[n % SLOTS]
        vz = in_direction(direction, v)
        if kind == "G":
            own_wait(s, vz, x, core)
            own_send(s, vz, x, MATE, mate)
        elif kind == "H":
            near_wait(s, vz, core)
            near_send(s, vz, MATE - 1, mate)
        elif kind == "R1":
            at = landing(direction, zz, vz)
            arrive(z1i.at[s, at], m["z1_r"].at[s, at])
        else:
            at = landing(direction, zz, vz)
            arrive(z0i.at[s, at], m["z0_r"].at[s, at])

    def x_sum(s, v):
        arrive(m0i.at[s, 1, v], m["m0_r"].at[s, 1, v])
        p0[s, 0, 1, v] = p0[s, 0, 1, v] + m0i[s, 1, v]
        go(lambda: remote(p0.at[s, 0, 1, v], x0i.at[s, v], m["x0_s"].at[s, v], m["x0_r"].at[s, v], across))

    def x_near(s, zz):
        arrive(m1i.at[s, zz], m["m1_r"].at[s, zz])
        value = p1[s, 0, zz] + m1i[s, zz]
        if zz > 0:
            value = value + z1i[s, zz]
        if zz < Z - 1:
            value = value + z1i[s, Z]
        p1[s, 0, zz] = value
        go(lambda: remote(p1.at[s, 0, zz], x1i.at[s], m["x1_s"].at[s], m["x1_r"].at[s], across))

    def x_step(s, n, zz):
        near_first = order_static(zz)
        if n in (1, 3, 5):
            own_send(s, near_first[(n + 1) // 2], x, ACROSS, across)
        elif n in (2, 4, 6):
            x_sum(s, near_first[3 - n // 2])
        else:
            x_near(s, zz)

    def x_arrival(s, t, zz):
        v = order_static(zz)[t]
        own_wait(s, v, x_other, core)
        own_send(s, v, x_other, MATE, mate)

    def events(step):
        for zz in range(Z):
            log[0] = by_z[zz]

            @pl.when(z == zz)
            def _():
                for direction in (UP, DOWN):
                    if in_direction(direction, zz) > 0 and 0 <= step - 1 < STAGES * SLOTS:
                        z_arrival(direction, zz, step - 1)
                for direction in (UP, DOWN):
                    if in_direction(direction, zz) < Z - 1 and 2 <= step + 1 < STAGES * SLOTS:
                        z_send(direction, zz, step + 1)
                for s in range(STAGES):
                    n = step - SLOTS * s
                    if 1 <= n <= 7:
                        x_step(s, n, zz)
                    if n in (2, 3, 5, 7):
                        x_arrival(s, (0, 0, 0, 1, 0, 2, 0, 3)[n] if n > 2 else 0, zz)

            log[0] = common

    def begin(s):
        own_send(s, z, x, ACROSS, across)
        own_send(s, z, x, MATE, mate)
        near_send(s, z, MATE - 1, mate)

    for zz in range(Z):
        log[0] = by_z[zz]

        @pl.when(z == zz)
        def _():
            for direction in (UP, DOWN):
                if in_direction(direction, zz) < Z - 1:
                    z_send(direction, zz, 0)

        log[0] = common
    own_send(0, z, x, ACROSS, across)
    own_send(0, z, x, MATE, mate)

    mask(near_tiles[0])
    near[0, z, core_rows(core), :] = fac[:, columns(near_tiles[0])]
    near_send(0, z, MATE - 1, mate)
    for zz in range(Z):
        log[0] = by_z[zz]

        @pl.when(z == zz)
        def _():
            for direction in (UP, DOWN):
                if in_direction(direction, zz) < Z - 1:
                    z_send(direction, zz, 1)

        log[0] = common

    for t in (sum_tiles[0], sum_tiles[1], near_tiles[1], own_tiles[1]):
        mask(t)
    for n, t in enumerate((sum_tiles[0], sum_tiles[1], near_tiles[0], near_tiles[1])):
        high, low = split(fac[:, columns(t)])
        lr_hi[:, columns(n)] = high
        lr_lo[:, columns(n)] = low

    def chip_job(q):
        v = order(3 - q // 2)
        other = q % 2 == 0
        side = 1 if other else 0
        chip = job_chip(q)
        load_anc(q).wait()

        def both(i, carry):
            c = core + (1 - 2 * core) * (1 - i)
            pair = split(a_buf[q % 4, core_rows(c), :])
            count = (4 if other else 2) * tile
            value = dot3(pair, (lr_hi[:, :count], lr_lo[:, :count]))
            for s in range(STAGES):
                p0[s, 1 - i, side, v] = value[:, columns(s)]
                if other:
                    p1[s, 1 - i, v] = value[:, columns(2 + s)]
            return carry

        lax.fori_loop(0, 2, both, 0)
        for s in range(STAGES):
            go(lambda s=s: remote(p0.at[s, 1, side, v], m0i.at[s, side, v], m["m0_s"].at[s, side, v], m["m0_r"].at[s, side, v], mate))
            if other:
                go(lambda s=s: remote(p1.at[s, 1, v], m1i.at[s, v], m["m1_s"].at[s, v], m["m1_r"].at[s, v], mate))

        def flip(c, carry):
            high, low = split(a_buf[q % 4, core_rows(c), :].T)
            at = pl.ds(pl.multiple_of(c * rows, rows), rows)
            tr_hi[chip, :, at] = high
            tr_lo[chip, :, at] = low
            return carry

        lax.fori_loop(0, 2, flip, 0)
        if q + 4 < 8:
            load_anc(q + 4).start()

    def pair_job(block, total, chip, first):
        high, low = split(block)
        left, rest = tr_hi[chip], tr_lo[chip]
        wide = jnp.dot(left, jnp.concatenate([high, low], axis=1), preferred_element_type=jnp.float32)
        value = wide[:, :tile] + (wide[:, tile:] + jnp.dot(rest, high, preferred_element_type=jnp.float32))
        if first:
            total[...] = value
        else:
            total[...] += value

    def own_job(s, t, other):
        zz = order(t)
        xx = 1 - x if other else x
        own_wait(s, zz, xx, 1 - core)
        pair_job(own[s, zz * 2 + xx], y_own.at[s], zz * 2 + xx, t == 0 and not other)

    def near_job(s, t):
        zz = order(t)
        near_wait(s, zz, 1 - core)
        pair_job(near[s, zz], y_near.at[s], zz * 2 + x, t == 0)

    def finish(s):
        cols_ref[:, columns(own_tiles[s])] = y_own[s]
        arrive(x1i.at[s], m["x1_r"].at[s])
        cols_ref[:, columns(near_tiles[s])] = y_near[s] + x1i[s]
        arrive(m0i.at[s, 0, z], m["m0_r"].at[s, 0, z])
        arrive(x0i.at[s, z], m["x0_r"].at[s, z])
        value = p0[s, 0, 0, z] + m0i[s, 0, z] + x0i[s, z]
        low = z0i[s, z]
        high = z0i[s, Z]
        value = value + jnp.where(z > 0, low, 0.0) + jnp.where(z < Z - 1, high, 0.0)
        cols_ref[:, columns(sum_tiles[s])] = value

    half_cols = 3 * tile
    sum_list = (
        [(q, p) for q in (3, 4, 5) for p in range(q + 1)],
        [(q, p) for q in (0, 1, 2) for p in range(q + 1)],
    )

    def inner_early():
        flipped = split(cols_ref[:, half_cols:].T)
        value = dot3(flipped, split(fac[...]))
        for n, (q, p) in enumerate(sum_list[0]):
            m["part0"][n] = value[(q - 3) * tile : (q - 2) * tile, columns(p)]

    def inner_late():
        value = dot3((lt_hi[...], lt_lo[...]), split(cols_ref[:, :half_cols]))
        for n, (q, p) in enumerate(sum_list[1]):
            m["part1"][n] = value[columns(q), columns(p)]

    groups = {
        "mate": (2, core, lambda n: index(z, x, n)),
        "x": (2, x, lambda n: index(z, n, core)),
        "z": (Z, z, lambda n: index(n, x, core)),
        "lane": (LANES, lane, lambda n: n * 2 + core),
    }

    def reducer(s):
        plan = LEVELS[s]
        sums = m[f"sum{s}"]
        sizes = [tile]
        for name in plan:
            sizes.append(sizes[-1] // groups[name][0])
        base = [0]
        for name, size in zip(plan, sizes[1:]):
            base.append(base[-1] + groups[name][1] * size)

        def held(level):
            return m[f"part{s}"] if level == 0 else m[f"held{s}_{level}"]

        def peer_of(level, d):
            count, mine, _ = groups[plan[level]]
            return 1 - mine if count == 2 else lax.rem(mine + d, count)

        def send_down(level):
            count, mine, device = groups[plan[level]]
            size = sizes[level + 1]
            for d in range(1, count):
                def make(d=d):
                    peer = peer_of(level, d)
                    src = held(level).at[:, pl.ds(pl.multiple_of(peer * size, size), size), :]
                    return remote(
                        src, m[f"slot{s}_{level}"].at[mine], m[f"ds{s}"].at[level, peer], m[f"dr{s}"].at[level, mine], device(peer)
                    )
                go(make)

        def take_down(level):
            count, mine, device = groups[plan[level]]
            size = sizes[level + 1]
            slot = m[f"slot{s}_{level}"]
            total = held(level)[:, pl.ds(pl.multiple_of(mine * size, size), size), :]
            for d in range(1, count):
                peer = peer_of(level, d)
                arrive(slot.at[peer], m[f"dr{s}"].at[level, peer])
                total = total + slot[peer]
            if level + 1 < len(plan):
                held(level + 1)[...] = total
            else:
                sums[:, pl.ds(pl.multiple_of(base[-1], size), size), :] = total

        def part_at(level, owner):
            size = sizes[level + 1]
            return sums.at[:, pl.ds(pl.multiple_of(base[level] + owner * size, size), size), :]

        def send_up(level):
            count, mine, device = groups[plan[level]]
            for d in range(1, count):
                def make(d=d):
                    peer = peer_of(level, d)
                    ref = part_at(level, mine)
                    return remote(ref, ref, m[f"us{s}"].at[level, peer], m[f"ur{s}"].at[level, mine], device(peer))
                go(make)

        def take_up(level):
            count, mine, device = groups[plan[level]]
            for d in range(1, count):
                peer = peer_of(level, d)
                arrive(part_at(level, peer), m[f"ur{s}"].at[level, peer])

        steps = [lambda: send_down(0)]
        for level in range(len(plan)):
            def step(level=level):
                take_down(level)
                if level + 1 < len(plan):
                    send_down(level + 1)
                else:
                    send_up(level)
            steps.append(step)
        for level in range(len(plan) - 1, -1, -1):
            def step(level=level):
                take_up(level)
                if level > 0:
                    send_up(level - 1)
            steps.append(step)
        return steps

    inner = m["inner"]
    blocks = [(2, 2), (2, 1), (2, 0), (1, 1), (1, 0), (0, 0)]

    def place(s):
        for n, (q, p) in enumerate(sum_list[s]):
            value = m[f"sum{s}"][n]
            at = blocks.index((q // 2, p // 2))
            inner[at, (q % 2) * tile : (q % 2 + 1) * tile, (p % 2) * tile : (p % 2 + 1) * tile] = value
            if q // 2 == p // 2 and q != p:
                inner[at, (p % 2) * tile : (p % 2 + 1) * tile, (q % 2) * tile : (q % 2 + 1) * tile] = value.T

    def n_block(j, k):
        return inner[blocks.index((j, k))]

    def fac_block(j, k):
        return win_st[win_pairs.index((j, k))]

    def put(j, k, value):
        out_ref[j * width : (j + 1) * width, k * width : (k + 1) * width] = value

    def got(j, k):
        return out_ref[j * width : (j + 1) * width, k * width : (k + 1) * width]

    early = m["early"]

    def window_first():
        put(2, 2, piv_st[2] + n_block(2, 2))
        value = n_block(2, 1) - mul(got(2, 2), fac_block(2, 1))
        put(2, 1, value)
        put(1, 2, value.T)
        value = n_block(2, 0) - mul(got(2, 1), fac_block(1, 0)) - mul(got(2, 2), fac_block(2, 0))
        put(2, 0, value)
        put(0, 2, value.T)

    def window_second():
        flip21 = split(fac_block(2, 1).T)
        known = piv_st[1] - mul(n_block(2, 1).T, fac_block(2, 1)) - dot3(flip21, split(got(2, 1)))
        early[0] = known
        turned = dot3(flip21, split(n_block(2, 0)))
        left = jnp.concatenate([fac_block(2, 1).T, known, got(1, 2)], axis=1)
        right = jnp.concatenate([n_block(2, 0), fac_block(1, 0), fac_block(2, 0)], axis=0)
        early[1] = mul(left, right)
        early[2] = (
            piv_st[0]
            + mul(turned.T, fac_block(1, 0))
            - mul(n_block(2, 0).T, fac_block(2, 0))
            - mul(fac_block(2, 0).T, got(2, 0))
        )

    def window_last():
        put(1, 1, early[0] + n_block(1, 1))
        value = n_block(1, 0) - early[1] - mul(n_block(1, 1), fac_block(1, 0))
        put(1, 0, value)
        put(0, 1, value.T)
        put(0, 0, early[2] + n_block(0, 0) - mul(n_block(1, 0).T, fac_block(1, 0)) - mul(fac_block(1, 0).T, value))

    def column(k):
        return cols_ref[:, k * width : (k + 1) * width]

    def put_column(k):
        value = column(k)
        for j in range(k + 1, 3):
            value = value + mul(column(j), fac_block(j, k))
        cols_ref[:, k * width : (k + 1) * width] = -value

    chip_job(0)
    chip_job(1)
    x_sum(0, order(3))
    load_piv.start()
    for n in range(3):
        load_win(n).start()
    events(1)
    chip_job(2)
    chip_job(3)
    events(2)
    chip_job(4)
    chip_job(5)
    events(3)
    chip_job(6)
    chip_job(7)
    events(4)
    own[1, lane, core_rows(core), :] = fac[:, columns(own_tiles[1])]
    near[1, z, core_rows(core), :] = fac[:, columns(near_tiles[1])]
    own_job(0, 0, False)
    own_job(0, 1, False)
    events(5)
    near_job(0, 0)
    near_job(0, 1)
    own_job(0, 0, True)
    own_job(0, 1, True)
    events(6)
    own_job(0, 2, False)
    near_job(0, 2)
    own_job(0, 2, True)
    events(7)
    begin(1)
    x_sum(1, order(3))
    own_job(0, 3, False)
    high, low = split(fac[:, :half_cols].T)
    lt_hi[...] = high
    lt_lo[...] = low
    events(8)
    near_job(0, 3)
    own_job(0, 3, True)
    events(9)
    finish(0)
    inner_early()
    cols_ref[:, 2 * width :] = -cols_ref[:, 2 * width :]
    first, last = reducer(0), reducer(1)
    first[0]()
    events(10)
    first[1]()
    own_job(1, 0, False)
    own_job(1, 1, False)
    events(11)
    first[2]()
    near_job(1, 0)
    near_job(1, 1)
    own_job(1, 0, True)
    events(12)
    first[3]()
    own_job(1, 1, True)
    events(13)
    first[4]()
    own_job(1, 2, False)
    near_job(1, 2)
    events(14)
    first[5]()
    own_job(1, 2, True)
    load_piv.wait()
    for n in range(3):
        load_win(n).wait()
    events(15)
    first[6]()
    own_job(1, 3, False)
    place(0)
    window_first()
    near_job(1, 3)
    events(16)
    own_job(1, 3, True)
    finish(1)
    inner_late()
    last[0]()
    window_second()
    last[1]()
    put_column(1)
    last[2]()
    put_column(0)
    for step in last[3:]:
        step()
    place(1)
    window_last()

    for make in common:
        make().wait_send()
    for zz in range(Z):

        @pl.when(z == zz)
        def _():
            for make in by_z[zz]:
                make().wait_send()


LEVELS = (("mate", "x", "z"), ("mate", "lane"))
COUNT = dict(mate=2, x=2, z=Z, lane=LANES)


def fused(anc_inverse, anc_factor, win_factor, pivot_inverse, structure):
    steps, width = pivot_inverse.shape[:2]
    rows, all_cols = anc_factor.shape
    tile = width // 2
    f32, b16 = jnp.float32, jnp.bfloat16
    dma = pltpu.SemaphoreType.DMA
    block = (rows, tile)
    pair = (2 * rows, tile)
    spaces = dict(
        fac=pltpu.VMEM((rows, all_cols), f32),
        a_buf=pltpu.VMEM((4, 2 * rows, rows), f32),
        win=pltpu.VMEM((3, width, width), f32),
        piv=pltpu.VMEM(pivot_inverse.shape, f32),
        lr_hi=pltpu.VMEM((rows, 4 * tile), b16),
        lr_lo=pltpu.VMEM((rows, 4 * tile), b16),
        lt_hi=pltpu.VMEM((3 * tile, rows), b16),
        lt_lo=pltpu.VMEM((3 * tile, rows), b16),
        tr_hi=pltpu.VMEM((LANES, rows, 2 * rows), b16),
        tr_lo=pltpu.VMEM((LANES, rows, 2 * rows), b16),
        own=pltpu.VMEM((STAGES, LANES, *pair), f32),
        near=pltpu.VMEM((STAGES, Z, *pair), f32),
        y_own=pltpu.VMEM((STAGES, *block), f32),
        y_near=pltpu.VMEM((STAGES, *block), f32),
        p0=pltpu.VMEM((STAGES, 2, 2, Z, *block), f32),
        m0i=pltpu.VMEM((STAGES, 2, Z, *block), f32),
        x0i=pltpu.VMEM((STAGES, Z, *block), f32),
        z0i=pltpu.VMEM((STAGES, Z + 1, *block), f32),
        p1=pltpu.VMEM((STAGES, 2, Z, *block), f32),
        m1i=pltpu.VMEM((STAGES, Z, *block), f32),
        x1i=pltpu.VMEM((STAGES, *block), f32),
        z1i=pltpu.VMEM((STAGES, Z + 1, *block), f32),
        inner=pltpu.VMEM((6, width, width), f32),
        early=pltpu.VMEM((3, width, width), f32),
        load_sem=dma((13,)),
        own_s=dma((STAGES, 4, LANES)),
        own_r=dma((STAGES, LANES, 2)),
        near_s=dma((STAGES, 3, Z)),
        near_r=dma((STAGES, Z, 2)),
        m0_s=dma((STAGES, 2, Z)),
        m0_r=dma((STAGES, 2, Z)),
        x0_s=dma((STAGES, Z)),
        x0_r=dma((STAGES, Z)),
        z0_s=dma((STAGES, Z)),
        z0_r=dma((STAGES, Z + 1)),
        m1_s=dma((STAGES, Z)),
        m1_r=dma((STAGES, Z)),
        x1_s=dma((STAGES,)),
        x1_r=dma((STAGES,)),
        z1_s=dma((STAGES, Z)),
        z1_r=dma((STAGES, Z + 1)),
    )
    for s, plan in enumerate(LEVELS):
        tiles = (15, 6)[s]
        size = tile
        spaces[f"part{s}"] = pltpu.VMEM((tiles, tile, tile), f32)
        spaces[f"sum{s}"] = pltpu.VMEM((tiles, tile, tile), f32)
        for level, name in enumerate(plan):
            size //= COUNT[name]
            spaces[f"slot{s}_{level}"] = pltpu.VMEM((COUNT[name], tiles, size, tile), f32)
            if level + 1 < len(plan):
                spaces[f"held{s}_{level + 1}"] = pltpu.VMEM((tiles, size, tile), f32)
        for kind in ("ds", "dr", "us", "ur"):
            spaces[f"{kind}{s}"] = dma((len(plan), LANES))
    whole = pl.BlockSpec(memory_space=pl.ANY)
    vmem = pl.BlockSpec(memory_space=pltpu.VMEM)
    return pl.pallas_call(
        functools.partial(fused_kernel, tuple(spaces), width),
        out_shape=(
            jax.ShapeDtypeStruct((rows, all_cols), f32),
            jax.ShapeDtypeStruct((all_cols, all_cols), f32),
        ),
        in_specs=[whole, whole, whole, whole, pl.BlockSpec(memory_space=pltpu.SMEM)],
        out_specs=(vmem, vmem),
        scratch_shapes=list(spaces.values()),
        compiler_params=pltpu.CompilerParams(
            collective_id=0, has_side_effects=True, vmem_limit_bytes=63 * 2**20
        ),
    )(anc_inverse, anc_factor, win_factor, pivot_inverse, structure)


precise = lax.Precision.HIGHEST


def product(left, right):
    return jnp.dot(left, right, precision=precise, preferred_element_type=jnp.float32)


def on_device(anc_inverse, anc_factor, win_factor, pivot_inverse, structure):
    row_count = lax.axis_size("prow")
    col_count = lax.axis_size("pcol")
    steps, width = pivot_inverse.shape[:2]
    fits = steps == 3 and 2 * anc_factor.shape[0] == 3 * width and width % 256 == 0
    if row_count == 1 and col_count == 4 * Z and fits:
        return fused(anc_inverse, anc_factor, win_factor, pivot_inverse, structure)
    row_index = lax.axis_index("prow")
    col_index = lax.axis_index("pcol")
    block_rows = anc_inverse.shape[0]
    block_cols = anc_inverse.shape[1]
    steps_total = pivot_inverse.shape[0]
    width = pivot_inverse.shape[1]
    all_cols = anc_factor.shape[1]
    block_count = structure.shape[1]
    ratio_cols = col_count // row_count
    share_rows = block_rows // col_count
    structure_cols = structure.T.astype(jnp.float32)
    global_rows = col_index * block_cols + lax.iota(jnp.int32, block_cols)
    onehot_rows = (
        (global_rows // width)[:, None] == lax.iota(jnp.int32, block_count)[None, :]
    ).astype(jnp.float32)
    kept_rows = product(onehot_rows, structure_cols)
    share_offset = col_index * share_rows
    share_global = (row_index * col_count + col_index) * share_rows + lax.iota(
        jnp.int32, share_rows
    )
    onehot_share = (
        (share_global // width)[:, None] == lax.iota(jnp.int32, block_count)[None, :]
    ).astype(jnp.float32)
    kept_share = product(onehot_share, structure_cols)
    slot_ids = lax.iota(jnp.int32, col_count)
    source_flag = (slot_ids // row_count == col_index - row_index * ratio_cols).astype(jnp.float32)
    pieces = jnp.tile(anc_factor.reshape(row_count, share_rows, all_cols), (ratio_cols, 1, 1))
    outgoing = pieces * source_flag[:, None, None]
    incoming = lax.all_to_all(outgoing, "pcol", split_axis=0, concat_axis=0, tiled=True)
    factor_share = jnp.sum(incoming, axis=0)
    column_store = {}
    share_store = {}
    window_blocks = {}
    for k in range(steps_total - 1, -1, -1):
        first_col = k * width
        factor_now = anc_factor[:, first_col : first_col + width] * kept_rows[:, k : k + 1]
        share_factor = factor_share[:, first_col : first_col + width] * kept_share[:, k : k + 1]
        finished = list(range(k + 1, steps_total))
        if finished:
            stacked = jnp.concatenate([column_store[j] for j in finished], axis=1)
            factor_win = win_factor[first_col + width :, first_col : first_col + width]

        def term_rows(start, count, factor_now=factor_now):
            return product(anc_inverse, factor_now)

        share_image = lax.psum_scatter(
            term_rows(jnp.int32(0), share_rows * lax.axis_size("pcol")),
            "pcol",
            scatter_dimension=0,
            tiled=True,
        )
        if finished:
            share_image = share_image + product(
                lax.dynamic_slice_in_dim(stacked, share_offset, share_rows, 0), factor_win
            )
        share_column = -share_image
        column_now = lax.all_gather(share_column, "pcol", axis=0, tiled=True)
        crossings = [product(share_store[j].T, share_factor) for j in finished]
        pivot_part = product(share_factor.T, share_column)
        cross_sums = []
        if finished:
            cross_total = lax.psum(jnp.stack(crossings), ("prow", "pcol"))
            cross_sums = [cross_total[position] for position in range(len(finished))]
        pivot_sum = lax.psum(pivot_part, ("prow", "pcol"))
        for position, j in enumerate(finished):
            running = cross_sums[position]
            for i in finished:
                running = running + product(
                    window_blocks[j, i],
                    win_factor[i * width : (i + 1) * width, first_col : first_col + width],
                )
            window_blocks[j, k] = -running
            window_blocks[k, j] = -running.T
        pivot_block = pivot_inverse[k] - pivot_sum
        for j in finished:
            pivot_block = pivot_block - product(
                win_factor[j * width : (j + 1) * width, first_col : first_col + width].T,
                window_blocks[j, k],
            )
        window_blocks[k, k] = pivot_block
        column_store[k] = column_now
        share_store[k] = share_column
    anc_columns = jnp.concatenate([share_store[k] for k in range(steps_total)], axis=1)
    win_inverse = jnp.concatenate(
        [
            jnp.concatenate([window_blocks[i, k] for k in range(steps_total)], axis=1)
            for i in range(steps_total)
        ],
        axis=0,
    )
    return (anc_columns, win_inverse)


def solution(mesh):
    in_specs = (
        P(("pole", "prow"), "pcol"),
        P(("pole", "pcol"), None),
        P("pole", None),
        P("pole", None, None),
        P(),
    )
    out_specs = (P(("pole", "prow", "pcol"), None), P("pole", None))
    return jax.shard_map(
        on_device, mesh=mesh, in_specs=in_specs, out_specs=out_specs, check_vma=False
    )
```

time: 155 us -> 124 us (0.80)
  Pallas kernels: 150 us -> 119 us
    pallas_call x1, Pallas kernels: 150 us -> 119 us  [fused(): pl.pallas_call(functools.partial(fused_kernel, tuple(spaces), width), out...]
where the time goes in v1:
time: 124 us
  Pallas kernels  119 us (96%)
  local copies, waits for them, and re-layouts  3.92 us (3%)
    pallas_call x1, Pallas kernels, fused(): pl.pallas_call(functools.partial(fused_kernel, tuple(spaces), width), out...  119 us
    unnamed x4, local copies, waits for them, and re-layouts  3.92 us

profile of v1, /device:TPU:1, one launch (start us, length us, event | category | flops | bytes accessed | tf_op | source)
XLA Modules:
  0.0 123.6 jit_solution(10174286359433966075)
XLA Ops:
  0.6 119.0 %shard_map.68 = (f32[384,768]{1,0:T(8,128)}, f32[768,768]{1,0:T(8,128)}) custom-call(f32[6144,384]{1,0:T(8,128)} %anc_ref.1, f32[384,768]{1,0:T(8,128)} %fac_ref.1, f32[768,768]{1,0:T(8,128)} %win_ref.1, f32[3,256,256]{2,1,0:T(8,128)} %piv_ref.1, s32[3,24]{1,0:T(4,128)} %str_ref.1), custom_call_target="tpu_custom_call" | custom-call | tf_op jit(solution)/shard_map/pallas_call | solution.py:715
  119.7 0.0 copy-start
  119.7 2.5 %copy.9 = f32[384,768]{1,0:T(8,128)} copy(f32[384,768]{1,0:T(8,128)} %get-tuple-element.4) | data formatting | bytes 2359296
  122.2 0.0 copy-done
  122.2 1.4 %copy.10 = f32[768,768]{1,0:T(8,128)} copy(f32[768,768]{1,0:T(8,128)S(1)} %copy-done) | data formatting | bytes 4718592
Async XLA Ops:
  119.7 2.5 %copy-start = (f32[768,768]{1,0:T(8,128)S(1)}, f32[768,768]{1,0:T(8,128)}, u32[]{:S(2)}) copy-start(f32[768,768]{1,0:T(8,128)} %get-tuple-element.5) | copy-start | bytes 7077892

commit v2 on v1

--- a/solution.py
+++ b/solution.py
@@ -30,26 +30,43 @@
 
 
 STAGES = 2
-SLOTS = 8
-
-
-def item_list(u):
+FIRST = (0, 9)
+TOTAL = 17
+
+
+def item_list(s, u):
     if u == 0:
         rest = [("R1", 3), ("R0", 3), ("R1", 2), ("R0", 2), ("R1", 1), ("R0", 1)]
         return [("G", 0), ("H", 0)] + rest
+    far = [("X", 0)] if s == 0 else []
     if u == 1:
-        rest = [("R1", 3), ("R0", 3), ("R1", 2), ("R0", 2)]
+        rest = [("R1", 3)] + far + [("R0", 3), ("R1", 2), ("R0", 2)]
         return [("G", 1), ("H", 1), ("G", 0), ("H", 0)] + rest
-    rest = [("G", 1), ("H", 1), ("G", 0), ("H", 0), ("R1", 3), ("R0", 3)]
+    rest = [("G", 1), ("H", 1), ("G", 0), ("H", 0), ("R1", 3)] + far + [("R0", 3)]
     return [("G", 2), ("H", 2)] + rest
+
+
+def item_at(u, n):
+    s = 1 if n >= FIRST[1] else 0
+    items = item_list(s, u)
+    n -= FIRST[s]
+    return (s, *items[n]) if n < len(items) else (s, "", 0)
+
+
+X_SENDS = {
+    1: ("G", 0, 1), 2: ("F", 0, 2), 3: ("G", 0, 2), 4: ("F", 0, 1), 5: ("F", 0, 0), 7: ("F", 1, 3), 8: ("R", 0, 0),
+    9: ("F", 1, 2), 10: ("G", 1, 1), 11: ("F", 1, 1), 12: ("G", 1, 2), 13: ("F", 1, 0), 14: ("G", 1, 3), 16: ("R", 1, 0),
+}
+X_TAKES = {2: (0, 0), 3: (0, 1), 5: (0, 2), 9: (1, 0), 12: (1, 1), 14: (1, 2), 16: (1, 3)}
 
 
 def order_static(z):
     return ([0, 1, 2, 3], [1, 0, 2, 3], [2, 3, 1, 0], [3, 2, 1, 0])[z]
 
 
-def fused_kernel(names, width, anc_ref, fac_ref, win_ref, piv_ref, str_ref, cols_ref, out_ref, *scratch):
+def fused_kernel(names, width, anc_ref, fac_ref, win_ref, piv_ref, str_ref, cols_hbm, out_hbm, *scratch):
     m = dict(zip(names, scratch, strict=True))
+    cols_ref, out_ref = m["cols"], m["out"]
     fac, a_buf, win_st, piv_st = m["fac"], m["a_buf"], m["win"], m["piv"]
     lr_hi, lr_lo, lt_hi, lt_lo = m["lr_hi"], m["lr_lo"], m["lt_hi"], m["lt_lo"]
     tr_hi, tr_lo = m["tr_hi"], m["tr_lo"]
@@ -176,7 +193,7 @@
         return Z if direction == DOWN and dest_z == zz else dest_z
 
     def z_send(direction, zz, n):
-        s, (kind, v) = n // SLOTS, item_list(in_direction(direction, zz))[n % SLOTS]
+        s, kind, v = item_at(in_direction(direction, zz), n)
         vz = in_direction(direction, v)
         first = in_direction(direction, zz) == 0
         dest = z_dest(direction)
@@ -185,6 +202,8 @@
             own_send(s, vz, x, direction, dest)
         elif kind == "H":
             near_send(s, vz, direction, dest)
+        elif kind == "X":
+            own_send(s, vz, x_other, direction, dest)
         elif kind == "R1":
             arrive(m1i.at[s, vz], m["m1_r"].at[s, vz])
             value = p1[s, 0, vz] + m1i[s, vz]
@@ -193,7 +212,7 @@
             p1[s, 0, vz] = value
             at = landing(direction, there, vz)
             go(lambda: remote(p1.at[s, 0, vz], z1i.at[s, at], m["z1_s"].at[s, vz], m["z1_r"].at[s, at], z_dest(direction)))
-        else:
+        elif kind == "R0":
             arrive(m0i.at[s, 0, vz], m["m0_r"].at[s, 0, vz])
             arrive(x0i.at[s, vz], m["x0_r"].at[s, vz])
             value = p0[s, 0, 0, vz] + m0i[s, 0, vz] + x0i[s, vz]
@@ -205,7 +224,7 @@
 
     def z_arrival(direction, zz, n):
         u = in_direction(direction, zz)
-        s, (kind, v) = n // SLOTS, item_list(u - 1)[n % SLOTS]
+        s, kind, v = item_at(u - 1, n)
         vz = in_direction(direction, v)
         if kind == "G":
             own_wait(s, vz, x, core)
@@ -213,10 +232,13 @@
         elif kind == "H":
             near_wait(s, vz, core)
             near_send(s, vz, MATE - 1, mate)
+        elif kind == "X":
+            own_wait(s, vz, x_other, core)
+            own_send(s, vz, x_other, MATE, mate)
         elif kind == "R1":
             at = landing(direction, zz, vz)
             arrive(z1i.at[s, at], m["z1_r"].at[s, at])
-        else:
+        elif kind == "R0":
             at = landing(direction, zz, vz)
             arrive(z0i.at[s, at], m["z0_r"].at[s, at])
 
@@ -235,12 +257,12 @@
         p1[s, 0, zz] = value
         go(lambda: remote(p1.at[s, 0, zz], x1i.at[s], m["x1_s"].at[s], m["x1_r"].at[s], across))
 
-    def x_step(s, n, zz):
-        near_first = order_static(zz)
-        if n in (1, 3, 5):
-            own_send(s, near_first[(n + 1) // 2], x, ACROSS, across)
-        elif n in (2, 4, 6):
-            x_sum(s, near_first[3 - n // 2])
+    def x_step(kind, s, t, zz):
+        v = order_static(zz)[t]
+        if kind == "G":
+            own_send(s, v, x, ACROSS, across)
+        elif kind == "F":
+            x_sum(s, v)
         else:
             x_near(s, zz)
 
@@ -256,17 +278,15 @@
             @pl.when(z == zz)
             def _():
                 for direction in (UP, DOWN):
-                    if in_direction(direction, zz) > 0 and 0 <= step - 1 < STAGES * SLOTS:
+                    if in_direction(direction, zz) > 0 and 0 <= step - 1 < TOTAL:
                         z_arrival(direction, zz, step - 1)
                 for direction in (UP, DOWN):
-                    if in_direction(direction, zz) < Z - 1 and 2 <= step + 1 < STAGES * SLOTS:
+                    if in_direction(direction, zz) < Z - 1 and 2 <= step + 1 < TOTAL:
                         z_send(direction, zz, step + 1)
-                for s in range(STAGES):
-                    n = step - SLOTS * s
-                    if 1 <= n <= 7:
-                        x_step(s, n, zz)
-                    if n in (2, 3, 5, 7):
-                        x_arrival(s, (0, 0, 0, 1, 0, 2, 0, 3)[n] if n > 2 else 0, zz)
+                if step in X_SENDS:
+                    x_step(*X_SENDS[step], zz)
+                if step in X_TAKES:
+                    x_arrival(*X_TAKES[step], zz)
 
             log[0] = common
 
@@ -365,8 +385,10 @@
         near_wait(s, zz, 1 - core)
         pair_job(near[s, zz], y_near.at[s], zz * 2 + x, t == 0)
 
+    def finish_own(s):
+        cols_ref[:, columns(own_tiles[s])] = y_own[s]
+
     def finish(s):
-        cols_ref[:, columns(own_tiles[s])] = y_own[s]
         arrive(x1i.at[s], m["x1_r"].at[s])
         cols_ref[:, columns(near_tiles[s])] = y_near[s] + x1i[s]
         arrive(m0i.at[s, 0, z], m["m0_r"].at[s, 0, z])
@@ -380,7 +402,8 @@
     half_cols = 3 * tile
     sum_list = (
         [(q, p) for q in (3, 4, 5) for p in range(q + 1)],
-        [(q, p) for q in (0, 1, 2) for p in range(q + 1)],
+        [(2, p) for p in range(3)],
+        [(q, p) for q in (0, 1) for p in range(q + 1)],
     )
 
     def inner_early():
@@ -389,10 +412,15 @@
         for n, (q, p) in enumerate(sum_list[0]):
             m["part0"][n] = value[(q - 3) * tile : (q - 2) * tile, columns(p)]
 
+    def inner_middle():
+        value = dot3(split(cols_ref[:, columns(2)].T), split(fac[:, :half_cols]))
+        for n, (q, p) in enumerate(sum_list[1]):
+            m["part1"][n] = value[:, columns(p)]
+
     def inner_late():
-        value = dot3((lt_hi[...], lt_lo[...]), split(cols_ref[:, :half_cols]))
-        for n, (q, p) in enumerate(sum_list[1]):
-            m["part1"][n] = value[columns(q), columns(p)]
+        value = dot3((lt_hi[:width, :], lt_lo[:width, :]), split(cols_ref[:, :width]))
+        for n, (q, p) in enumerate(sum_list[2]):
+            m["part2"][n] = value[columns(q), columns(p)]
 
     groups = {
         "mate": (2, core, lambda n: index(z, x, n)),
@@ -497,8 +525,18 @@
     def fac_block(j, k):
         return win_st[win_pairs.index((j, k))]
 
+    def save_block(j, k):
+        block = out_ref.at[pl.ds(j * width, width), pl.ds(k * width, width)]
+        target = out_hbm.at[pl.ds(j * width, width), pl.ds(k * width, width)]
+        return pltpu.make_async_copy(block, target, m["save_sem"].at[j, k])
+
+    def save_column(k):
+        at = pl.ds(k * width, width)
+        return pltpu.make_async_copy(cols_ref.at[:, at], cols_hbm.at[:, at], m["save_sem"].at[3, k])
+
     def put(j, k, value):
         out_ref[j * width : (j + 1) * width, k * width : (k + 1) * width] = value
+        save_block(j, k).start()
 
     def got(j, k):
         return out_ref[j * width : (j + 1) * width, k * width : (k + 1) * width]
@@ -557,12 +595,12 @@
     events(2)
     chip_job(4)
     chip_job(5)
+    own[1, lane, core_rows(core), :] = fac[:, columns(own_tiles[1])]
+    near[1, z, core_rows(core), :] = fac[:, columns(near_tiles[1])]
     events(3)
     chip_job(6)
     chip_job(7)
     events(4)
-    own[1, lane, core_rows(core), :] = fac[:, columns(own_tiles[1])]
-    near[1, z, core_rows(core), :] = fac[:, columns(near_tiles[1])]
     own_job(0, 0, False)
     own_job(0, 1, False)
     events(5)
@@ -571,67 +609,83 @@
     own_job(0, 0, True)
     own_job(0, 1, True)
     events(6)
+    begin(1)
     own_job(0, 2, False)
     near_job(0, 2)
     own_job(0, 2, True)
     events(7)
-    begin(1)
-    x_sum(1, order(3))
     own_job(0, 3, False)
     high, low = split(fac[:, :half_cols].T)
     lt_hi[...] = high
     lt_lo[...] = low
     events(8)
     near_job(0, 3)
+    events(9)
     own_job(0, 3, True)
-    events(9)
+    events(10)
+    finish_own(0)
     finish(0)
     inner_early()
     cols_ref[:, 2 * width :] = -cols_ref[:, 2 * width :]
-    first, last = reducer(0), reducer(1)
+    save_column(2).start()
+    first, middle, last = reducer(0), reducer(1), reducer(2)
     first[0]()
-    events(10)
+    own_job(1, 0, False)
     first[1]()
-    own_job(1, 0, False)
+    events(11)
     own_job(1, 1, False)
-    events(11)
-    first[2]()
     near_job(1, 0)
     near_job(1, 1)
     own_job(1, 0, True)
     events(12)
+    first[2]()
+    events(13)
     first[3]()
     own_job(1, 1, True)
-    events(13)
-    first[4]()
     own_job(1, 2, False)
     near_job(1, 2)
     events(14)
-    first[5]()
+    first[4]()
     own_job(1, 2, True)
     load_piv.wait()
     for n in range(3):
         load_win(n).wait()
     events(15)
+    first[5]()
+    own_job(1, 3, False)
+    events(16)
+    near_job(1, 3)
+    own_job(1, 3, True)
+    finish_own(1)
+    inner_middle()
+    middle[0]()
     first[6]()
-    own_job(1, 3, False)
     place(0)
     window_first()
-    near_job(1, 3)
-    events(16)
-    own_job(1, 3, True)
+    middle[1]()
+    events(17)
     finish(1)
     inner_late()
     last[0]()
+    middle[2]()
     window_second()
     last[1]()
+    middle[3]()
     put_column(1)
+    save_column(1).start()
     last[2]()
+    middle[4]()
     put_column(0)
+    save_column(0).start()
     for step in last[3:]:
         step()
     place(1)
+    place(2)
     window_last()
+    for k in range(3):
+        save_column(k).wait()
+        for j in range(3):
+            save_block(j, k).wait()
 
     for make in common:
         make().wait_send()
@@ -643,7 +697,7 @@
                 make().wait_send()
 
 
-LEVELS = (("mate", "x", "z"), ("mate", "lane"))
+LEVELS = (("mate", "x", "z"), ("mate", "lane"), ("mate", "lane"))
 COUNT = dict(mate=2, x=2, z=Z, lane=LANES)
 
 
@@ -656,6 +710,9 @@
     block = (rows, tile)
     pair = (2 * rows, tile)
     spaces = dict(
+        cols=pltpu.VMEM((rows, all_cols), f32),
+        out=pltpu.VMEM((all_cols, all_cols), f32),
+        save_sem=dma((4, 3)),
         fac=pltpu.VMEM((rows, all_cols), f32),
         a_buf=pltpu.VMEM((4, 2 * rows, rows), f32),
         win=pltpu.VMEM((3, width, width), f32),
@@ -699,7 +756,7 @@
         z1_r=dma((STAGES, Z + 1)),
     )
     for s, plan in enumerate(LEVELS):
-        tiles = (15, 6)[s]
+        tiles = (15, 3, 3)[s]
         size = tile
         spaces[f"part{s}"] = pltpu.VMEM((tiles, tile, tile), f32)
         spaces[f"sum{s}"] = pltpu.VMEM((tiles, tile, tile), f32)
@@ -711,7 +768,6 @@
         for kind in ("ds", "dr", "us", "ur"):
             spaces[f"{kind}{s}"] = dma((len(plan), LANES))
     whole = pl.BlockSpec(memory_space=pl.ANY)
-    vmem = pl.BlockSpec(memory_space=pltpu.VMEM)
     return pl.pallas_call(
         functools.partial(fused_kernel, tuple(spaces), width),
         out_shape=(
@@ -719,12 +775,44 @@
             jax.ShapeDtypeStruct((all_cols, all_cols), f32),
         ),
         in_specs=[whole, whole, whole, whole, pl.BlockSpec(memory_space=pltpu.SMEM)],
-        out_specs=(vmem, vmem),
+        out_specs=(whole, whole),
         scratch_shapes=list(spaces.values()),
         compiler_params=pltpu.CompilerParams(
             collective_id=0, has_side_effects=True, vmem_limit_bytes=63 * 2**20
         ),
     )(anc_inverse, anc_factor, win_factor, pivot_inverse, structure)
+
+
+def land_kernel(parts, *refs):
+    count = len(parts)
+    sources, targets = refs[:count], refs[count : 2 * count]
+    held, sem = refs[2 * count : 3 * count], refs[3 * count]
+    copies = []
+    for n, pieces in enumerate(parts):
+        size = sources[n].shape[0] // pieces
+        for i in range(pieces):
+            at = pl.ds(i * size, size)
+            read = pltpu.make_async_copy(sources[n].at[at, :], held[n].at[at, :], sem.at[0, len(copies)])
+            write = pltpu.make_async_copy(held[n].at[at, :], targets[n].at[at, :], sem.at[1, len(copies)])
+            read.start()
+            copies.append((read, write))
+    for read, write in copies:
+        read.wait()
+        write.start()
+    for read, write in copies:
+        write.wait()
+
+
+def land(*arrays):
+    whole = pl.BlockSpec(memory_space=pl.ANY)
+    parts = (3, 6)
+    return pl.pallas_call(
+        functools.partial(land_kernel, parts),
+        out_shape=tuple(jax.ShapeDtypeStruct(a.shape, a.dtype) for a in arrays),
+        in_specs=[whole] * len(arrays),
+        out_specs=(whole,) * len(arrays),
+        scratch_shapes=[pltpu.VMEM(a.shape, a.dtype) for a in arrays] + [pltpu.SemaphoreType.DMA((2, sum(parts)))],
+    )(*arrays)
 
 
 precise = lax.Precision.HIGHEST
@@ -740,7 +828,7 @@
     steps, width = pivot_inverse.shape[:2]
     fits = steps == 3 and 2 * anc_factor.shape[0] == 3 * width and width % 256 == 0
     if row_count == 1 and col_count == 4 * Z and fits:
-        return fused(anc_inverse, anc_factor, win_factor, pivot_inverse, structure)
+        return land(*fused(anc_inverse, anc_factor, win_factor, pivot_inverse, structure))
     row_index = lax.axis_index("prow")
     col_index = lax.axis_index("pcol")
     block_rows = anc_inverse.shape[0]

time: 124 us -> 118 us (0.952)
  local copies, waits for them, and re-layouts: 3.92 us -> 0 us
  Pallas kernels: 119 us -> 117 us
    pallas_call x1, Pallas kernels: 119 us -> 114 us  [fused(): pl.pallas_call(functools.partial(fused_kernel, tuple(spaces), width), out...]
    unnamed x4 -> x0, local copies, waits for them, and re-layouts: 3.92 us -> none
    pallas_call x0 -> x1, Pallas kernels: none -> 2.97 us  [land(): pl.pallas_call(functools.partial(land_kernel, parts), out_shape=tuple((ja...]
where the time goes in v2:
time: 118 us
  Pallas kernels  117 us (99%)
    pallas_call x1, Pallas kernels, fused(): pl.pallas_call(functools.partial(fused_kernel, tuple(spaces), width), out...  114 us
    pallas_call x1, Pallas kernels, land(): pl.pallas_call(functools.partial(land_kernel, parts), out_shape=tuple((ja...  2.97 us

profile of v2, /device:TPU:1, one launch (start us, length us, event | category | flops | bytes accessed | tf_op | source)
XLA Modules:
  0.0 117.9 jit_solution(5526954309360344960)
XLA Ops:
  0.6 114.1 %shard_map.68 = (f32[384,768]{1,0:T(8,128)}, f32[768,768]{1,0:T(8,128)}) custom-call(f32[6144,384]{1,0:T(8,128)} %anc_ref.1, f32[384,768]{1,0:T(8,128)} %fac_ref.1, f32[768,768]{1,0:T(8,128)} %win_ref.1, f32[3,256,256]{2,1,0:T(8,128)} %piv_ref.1, s32[3,24]{1,0:T(4,128)} %str_ref.1), custom_call_target="tpu_custom_call" | custom-call | tf_op jit(solution)/shard_map/pallas_call | solution.py:771
  114.8 3.0 %shard_map.69 = (f32[384,768]{1,0:T(8,128)}, f32[768,768]{1,0:T(8,128)}) custom-call(f32[384,768]{1,0:T(8,128)} %get-tuple-element.4.refs_0_, f32[768,768]{1,0:T(8,128)} %get-tuple-element.5.refs_1_), custom_call_target="tpu_custom_call" | custom-call | tf_op jit(solution)/shard_map/pallas_call | solution.py:809

commit v3 on v2

--- a/solution.py
+++ b/solution.py
@@ -640,18 +640,16 @@
     events(12)
     first[2]()
     events(13)
-    first[3]()
     own_job(1, 1, True)
     own_job(1, 2, False)
     near_job(1, 2)
     events(14)
-    first[4]()
+    first[3]()
     own_job(1, 2, True)
     load_piv.wait()
     for n in range(3):
         load_win(n).wait()
     events(15)
-    first[5]()
     own_job(1, 3, False)
     events(16)
     near_job(1, 3)
@@ -659,24 +657,26 @@
     finish_own(1)
     inner_middle()
     middle[0]()
-    first[6]()
-    place(0)
-    window_first()
     middle[1]()
     events(17)
     finish(1)
     inner_late()
     last[0]()
+    first[4]()
     middle[2]()
-    window_second()
-    last[1]()
-    middle[3]()
     put_column(1)
     save_column(1).start()
-    last[2]()
-    middle[4]()
+    last[1]()
     put_column(0)
     save_column(0).start()
+    first[5]()
+    middle[3]()
+    last[2]()
+    first[6]()
+    place(0)
+    window_first()
+    middle[4]()
+    window_second()
     for step in last[3:]:
         step()
     place(1)

time: 118 us -> 115 us (0.975)
  Pallas kernels: 117 us -> 114 us
    pallas_call x1, Pallas kernels: 114 us -> 111 us  [fused(): pl.pallas_call(functools.partial(fused_kernel, tuple(spaces), width), out...]
where the time goes in v3:
time: 115 us; the launch traced here: 114 us
  Pallas kernels  114 us (99%)
    pallas_call x1, Pallas kernels, fused(): pl.pallas_call(functools.partial(fused_kernel, tuple(spaces), width), out...  111 us
    pallas_call x1, Pallas kernels, land(): pl.pallas_call(functools.partial(land_kernel, parts), out_shape=tuple((ja...  2.97 us

profile of v3, /device:TPU:1, one launch (start us, length us, event | category | flops | bytes accessed | tf_op | source)
XLA Modules:
  0.0 114.4 jit_solution(5907810894363569785)
XLA Ops:
  0.6 110.6 %shard_map.68 = (f32[384,768]{1,0:T(8,128)}, f32[768,768]{1,0:T(8,128)}) custom-call(f32[6144,384]{1,0:T(8,128)} %anc_ref.1, f32[384,768]{1,0:T(8,128)} %fac_ref.1, f32[768,768]{1,0:T(8,128)} %win_ref.1, f32[3,256,256]{2,1,0:T(8,128)} %piv_ref.1, s32[3,24]{1,0:T(4,128)} %str_ref.1), custom_call_target="tpu_custom_call" | custom-call | tf_op jit(solution)/shard_map/pallas_call | solution.py:771
  111.2 3.0 %shard_map.69 = (f32[384,768]{1,0:T(8,128)}, f32[768,768]{1,0:T(8,128)}) custom-call(f32[384,768]{1,0:T(8,128)} %get-tuple-element.4.refs_0_, f32[768,768]{1,0:T(8,128)} %get-tuple-element.5.refs_1_), custom_call_target="tpu_custom_call" | custom-call | tf_op jit(solution)/shard_map/pallas_call | solution.py:809

commit v4 on v3

--- a/solution.py
+++ b/solution.py
@@ -30,15 +30,15 @@
 
 
 STAGES = 2
-FIRST = (0, 9)
-TOTAL = 17
+FIRST = (0, 8)
+TOTAL = 16
 
 
 def item_list(s, u):
     if u == 0:
         rest = [("R1", 3), ("R0", 3), ("R1", 2), ("R0", 2), ("R1", 1), ("R0", 1)]
         return [("G", 0), ("H", 0)] + rest
-    far = [("X", 0)] if s == 0 else []
+    far = []
     if u == 1:
         rest = [("R1", 3)] + far + [("R0", 3), ("R1", 2), ("R0", 2)]
         return [("G", 1), ("H", 1), ("G", 0), ("H", 0)] + rest
@@ -54,10 +54,10 @@
 
 
 X_SENDS = {
-    1: ("G", 0, 1), 2: ("F", 0, 2), 3: ("G", 0, 2), 4: ("F", 0, 1), 5: ("F", 0, 0), 7: ("F", 1, 3), 8: ("R", 0, 0),
-    9: ("F", 1, 2), 10: ("G", 1, 1), 11: ("F", 1, 1), 12: ("G", 1, 2), 13: ("F", 1, 0), 14: ("G", 1, 3), 16: ("R", 1, 0),
+    1: ("G", 0, 1), 2: ("F", 0, 2), 3: ("G", 0, 2), 4: ("F", 0, 1), 5: ("G", 0, 3), 6: ("F", 0, 0), 7: ("R", 0, 0), 8: ("F", 1, 3),
+    9: ("F", 1, 2), 10: ("G", 1, 1), 11: ("F", 1, 1), 12: ("G", 1, 2), 13: ("F", 1, 0), 14: ("G", 1, 3), 15: ("R", 1, 0),
 }
-X_TAKES = {2: (0, 0), 3: (0, 1), 5: (0, 2), 9: (1, 0), 12: (1, 1), 14: (1, 2), 16: (1, 3)}
+X_TAKES = {2: (0, 0), 3: (0, 1), 5: (0, 2), 7: (0, 3), 9: (1, 0), 12: (1, 1), 14: (1, 2), 16: (1, 3)}
 
 
 def order_static(z):
@@ -622,7 +622,6 @@
     near_job(0, 3)
     events(9)
     own_job(0, 3, True)
-    events(10)
     finish_own(0)
     finish(0)
     inner_early()
@@ -630,6 +629,7 @@
     save_column(2).start()
     first, middle, last = reducer(0), reducer(1), reducer(2)
     first[0]()
+    events(10)
     own_job(1, 0, False)
     first[1]()
     events(11)

time: 115 us -> 114 us (level)
  no operation moved by 1% of the time
where the time goes in v4:
time: 114 us
  Pallas kernels  113 us (99%)
    pallas_call x1, Pallas kernels, fused(): pl.pallas_call(functools.partial(fused_kernel, tuple(spaces), width), out...  110 us
    pallas_call x1, Pallas kernels, land(): pl.pallas_call(functools.partial(land_kernel, parts), out_shape=tuple((ja...  2.97 us

profile of v4, /device:TPU:1, one launch (start us, length us, event | category | flops | bytes accessed | tf_op | source)
XLA Modules:
  0.0 114.0 jit_solution(2411631752387676240)
XLA Ops:
  0.6 110.2 %shard_map.68 = (f32[384,768]{1,0:T(8,128)}, f32[768,768]{1,0:T(8,128)}) custom-call(f32[6144,384]{1,0:T(8,128)} %anc_ref.1, f32[384,768]{1,0:T(8,128)} %fac_ref.1, f32[768,768]{1,0:T(8,128)} %win_ref.1, f32[3,256,256]{2,1,0:T(8,128)} %piv_ref.1, s32[3,24]{1,0:T(4,128)} %str_ref.1), custom_call_target="tpu_custom_call" | custom-call | tf_op jit(solution)/shard_map/pallas_call | solution.py:771
  110.9 3.0 %shard_map.69 = (f32[384,768]{1,0:T(8,128)}, f32[768,768]{1,0:T(8,128)}) custom-call(f32[384,768]{1,0:T(8,128)} %get-tuple-element.4.refs_0_, f32[768,768]{1,0:T(8,128)} %get-tuple-element.5.refs_1_), custom_call_target="tpu_custom_call" | custom-call | tf_op jit(solution)/shard_map/pallas_call | solution.py:809

commit v5 on v4

--- a/solution.py
+++ b/solution.py
@@ -102,7 +102,10 @@
         at = pl.ds(pl.multiple_of(job_chip(q) * 2 * rows, 2 * rows), 2 * rows)
         return pltpu.make_async_copy(anc_ref.at[at, :], a_buf.at[q % 4], m["load_sem"].at[q])
 
-    load_fac = pltpu.make_async_copy(fac_ref, fac, m["load_sem"].at[8])
+    lead = pl.ds(5 * tile, tile)
+    load_lead = pltpu.make_async_copy(fac_ref.at[:, lead], fac.at[:, lead], m["load_sem"].at[8])
+    rest = pl.ds(0, 5 * tile)
+    load_fac = pltpu.make_async_copy(fac_ref.at[:, rest], fac.at[:, rest], m["load_sem"].at[13])
     load_piv = pltpu.make_async_copy(piv_ref, piv_st, m["load_sem"].at[9])
     win_pairs = [(2, 1), (1, 0), (2, 0)]
 
@@ -111,6 +114,7 @@
         block = win_ref.at[pl.ds(j * width, width), pl.ds(k * width, width)]
         return pltpu.make_async_copy(block, win_st.at[n], m["load_sem"].at[10 + n])
 
+    load_lead.start()
     load_fac.start()
     for q in range(4):
         load_anc(q).start()
@@ -176,7 +180,7 @@
 
     own_tiles, near_tiles, sum_tiles = (5, 2), (4, 1), (3, 0)
 
-    load_fac.wait()
+    load_lead.wait()
     mask(own_tiles[0])
     own[0, lane, core_rows(core), :] = fac[:, columns(own_tiles[0])]
     pl.semaphore_wait(barrier, LANES)
@@ -308,6 +312,7 @@
     own_send(0, z, x, ACROSS, across)
     own_send(0, z, x, MATE, mate)
 
+    load_fac.wait()
     mask(near_tiles[0])
     near[0, z, core_rows(core), :] = fac[:, columns(near_tiles[0])]
     near_send(0, z, MATE - 1, mate)
@@ -737,7 +742,7 @@
         z1i=pltpu.VMEM((STAGES, Z + 1, *block), f32),
         inner=pltpu.VMEM((6, width, width), f32),
         early=pltpu.VMEM((3, width, width), f32),
-        load_sem=dma((13,)),
+        load_sem=dma((14,)),
         own_s=dma((STAGES, 4, LANES)),
         own_r=dma((STAGES, LANES, 2)),
         near_s=dma((STAGES, 3, Z)),

time: 114 us -> 114 us (level)
  no operation moved by 1% of the time
where the time goes in v5:
time: 114 us
  Pallas kernels  113 us (99%)
    pallas_call x1, Pallas kernels, fused(): pl.pallas_call(functools.partial(fused_kernel, tuple(spaces), width), out...  110 us
    pallas_call x1, Pallas kernels, land(): pl.pallas_call(functools.partial(land_kernel, parts), out_shape=tuple((ja...  2.97 us

profile of v5, /device:TPU:1, one launch (start us, length us, event | category | flops | bytes accessed | tf_op | source)
XLA Modules:
  0.0 114.0 jit_solution(13923144653546193719)
XLA Ops:
  0.6 110.3 %shard_map.68 = (f32[384,768]{1,0:T(8,128)}, f32[768,768]{1,0:T(8,128)}) custom-call(f32[6144,384]{1,0:T(8,128)} %anc_ref.1, f32[384,768]{1,0:T(8,128)} %fac_ref.1, f32[768,768]{1,0:T(8,128)} %win_ref.1, f32[3,256,256]{2,1,0:T(8,128)} %piv_ref.1, s32[3,24]{1,0:T(4,128)} %str_ref.1), custom_call_target="tpu_custom_call" | custom-call | tf_op jit(solution)/shard_map/pallas_call | solution.py:776
  110.9 3.0 %shard_map.69 = (f32[384,768]{1,0:T(8,128)}, f32[768,768]{1,0:T(8,128)}) custom-call(f32[384,768]{1,0:T(8,128)} %get-tuple-element.4.refs_0_, f32[768,768]{1,0:T(8,128)} %get-tuple-element.5.refs_1_), custom_call_target="tpu_custom_call" | custom-call | tf_op jit(solution)/shard_map/pallas_call | solution.py:814
